TPU v7x, 32 devices: a whole 2x2x4 slice. The times are simulated.
32 devices in a mesh: pipe: 4 (over y, x), ctx: 8 (over z, core).
Axes of the slice: x: 2, y: 2, z: 4, core: 2. Of those that a mesh axis runs over, the one named last changes fastest.
Arguments:
- x_in: bfloat16 [4, 512, 8192], P('pipe', 'ctx'), may hold values from -6 to 6
- z_in: bfloat16 [4, 512, 8192], P('pipe', 'ctx'), may hold values from -6 to 6
- bc_in: bfloat16 [4, 512, 1024], P('pipe', 'ctx'), may hold values from -6 to 6
- dt_raw: bfloat16 [4, 512, 128], P('pipe', 'ctx'), may hold values from -3.2 to 3.2
- a_log: float32 [4, 128], P('pipe'), may hold values from -12 to 3
- dt_bias: float32 [4, 128], P('pipe'), may hold values from -3.8 to -3
- d_skip: float32 [4, 128], P('pipe'), may hold values from 0.5 to 1.5
- conv_x: bfloat16 [4, 4, 8192], P('pipe'), may hold values from -3 to 3
- conv_bc: bfloat16 [4, 4, 1024], P('pipe'), may hold values from -3 to 3
- norm_gain: float32 [4, 8192], P('pipe'), may hold values from 0.5 to 1.5
- seg_ids: int32 [4, 512], P('pipe', 'ctx'), may hold values from 0 to 3, never falling along the last dimension, each value on 1 to 256 neighbouring positions
- query: bfloat16 [4, 512, 2048], P('pipe', 'ctx'), may hold values from -192 to 192
- keys: bfloat16 [4, 512, 256], P('pipe', 'ctx'), may hold values from -6 to 6
- values: bfloat16 [4, 512, 256], P('pipe', 'ctx'), may hold values from -6 to 6
Outputs:
- mamba_out: bfloat16 [4, 512, 8192], P('pipe', 'ctx')
- handoff: bfloat16 [4, 512, 2048], P('pipe', 'ctx')
Inputs may be any that keep to these rules, and one draw needn't show every extreme that they name: `seg_ids`: segment numbers never fall along a section's sequence; no segment is longer than 256 positions, and one has exactly that many.
All inputs are finite; a program needn't handle non-finite values.
Results may differ from a plain program's by a relative error of at most 0.0044.
The roundings to bfloat16 on the way count: a program that leaves them out, or rounds other values in their place, can miss the bound.
Values may be sent and summed in bfloat16 or wider, within the bound.
No kernel may reach another device: no remote copies, remote signals or barrier semaphores. Data moves between devices by JAX's collectives and lax.ppermute only.
A program may use at most 128 MiB of HBM per device.

v0:
```python
import math
import jax
import jax.numpy as jnp
from jax import lax
from jax.sharding import PartitionSpec as P

G = 4
AH = 32
KVH = 4
HD = 64
norm_eps = 1e-05


def from_behind(value, axis, steps):
    count = lax.axis_size(axis)
    pairs = [(source, (source + steps) % count) for source in range(count)]
    return lax.ppermute(value, axis, pairs)


def causal_taps(rim, inputs, rim_ids, ids, weights):
    lag = rim.shape[0]
    length = inputs.shape[0]
    padded = jnp.concatenate([rim, inputs], axis=0)
    padded_ids = jnp.concatenate([rim_ids, ids])
    layout = (length,) + (1,) * (inputs.ndim - 1)
    summed = jnp.zeros(inputs.shape, jnp.float32)
    for tap in range(lag + 1):
        same = (padded_ids[tap : tap + length] == ids).reshape(layout)
        summed = summed + jnp.where(
            same,
            weights[tap].astype(jnp.float32) * padded[tap : tap + length].astype(jnp.float32),
            0.0,
        )
    return jax.nn.silu(summed).astype(jnp.bfloat16)


def per_head(grouped, heads):
    leading = grouped.shape[:-3]
    groups = grouped.shape[-2]
    states = grouped.shape[-1]
    moved = jnp.swapaxes(grouped, -3, -2)
    spread = jnp.repeat(moved, heads // groups, axis=-3)
    return spread.reshape(leading + (heads, 2 * states))


def state_space(x_conv, bc_conv, step_size, rates, skip, ids):
    length, local_heads, head_dim = x_conv.shape
    states = bc_conv.shape[2] // 2
    span = min(256, length)
    blocks = length // span
    lower = jnp.arange(span)[:, None] >= jnp.arange(span)[None, :]

    def advance(carry, item):
        memory, last_id = carry
        x_block, bc_block, step_block, id_block = item
        b_part = bc_block[:, :, :states]
        c_part = bc_block[:, :, states:]
        logs = jnp.cumsum(step_block * rates[None, :], axis=0)
        allowed = lower & (id_block[:, None] == id_block[None, :])
        gaps = logs[:, None, :] - logs[None, :, :]
        weights = (
            jnp.where(allowed[:, :, None], jnp.exp(jnp.minimum(gaps, 0.0)), 0.0)
            * step_block[None, :, :]
        )
        inner = jnp.einsum("thn,shn->tsh", c_part, b_part, preferred_element_type=jnp.float32)
        mixing = (inner * weights).astype(jnp.bfloat16)
        local_part = jnp.einsum("tsh,shp->thp", mixing, x_block, preferred_element_type=jnp.float32)
        keep = jnp.where((id_block == last_id)[:, None], jnp.exp(logs), 0.0)
        carried = (
            jnp.einsum(
                "thn,hpn->thp", c_part.astype(jnp.float32), memory, precision=lax.Precision.HIGHEST
            )
            * keep[:, :, None]
        )
        result = local_part + carried + skip[None, :, None] * x_block.astype(jnp.float32)
        tail = logs[span - 1]
        writes = (
            jnp.where((id_block == id_block[span - 1])[:, None], jnp.exp(tail[None, :] - logs), 0.0)
            * step_block
        )
        scaled = (x_block.astype(jnp.float32) * writes[:, :, None]).astype(jnp.bfloat16)
        added = jnp.einsum("shp,shn->hpn", scaled, b_part, preferred_element_type=jnp.float32)
        kept = jnp.where(id_block[span - 1] == last_id, jnp.exp(tail), 0.0)
        memory = memory * kept[:, None, None] + added
        return ((memory, id_block[span - 1]), result)

    start = (jnp.zeros((local_heads, head_dim, states), jnp.float32), jnp.array(-1, jnp.int32))
    items = (
        x_conv.reshape(blocks, span, local_heads, head_dim),
        bc_conv.reshape(blocks, span, local_heads, 2 * states),
        step_size.reshape(blocks, span, local_heads),
        ids.reshape(blocks, span),
    )
    (memory, _), outputs = lax.scan(advance, start, items)
    return (memory, outputs.reshape(length, local_heads, head_dim))


def on_device(
    x_in,
    z_in,
    bc_in,
    dt_raw,
    a_log,
    dt_bias,
    d_skip,
    conv_x,
    conv_bc,
    norm_gain,
    seg_ids,
    query,
    keys,
    values,
):
    ranks = lax.axis_size("ctx")
    place = lax.axis_index("ctx")
    tokens_here = x_in.shape[1]
    heads = dt_raw.shape[2]
    head_dim = x_in.shape[2] // heads
    states = bc_in.shape[2] // (2 * G)
    lag = conv_x.shape[1] - 1
    own_ids = seg_ids[0]
    all_ids = lax.all_gather(own_ids, "ctx", axis=0, tiled=True)
    local_heads = heads // ranks
    first_head = place * local_heads
    x_send = x_in[0].reshape(tokens_here, heads, head_dim)
    bc_send = per_head(bc_in[0].reshape(tokens_here, 2, G, states), heads)
    x_heads, raw_heads, bc_heads = (
        lax.all_to_all(x_send, "ctx", split_axis=1, concat_axis=0, tiled=True),
        lax.all_to_all(dt_raw[0], "ctx", split_axis=1, concat_axis=0, tiled=True),
        lax.all_to_all(bc_send, "ctx", split_axis=1, concat_axis=0, tiled=True),
    )
    empty_ids = jnp.full((lag,), -1, jnp.int32)
    taps_x = lax.dynamic_slice_in_dim(
        conv_x[0].reshape(lag + 1, heads, head_dim), first_head, local_heads, 1
    )
    taps_bc = lax.dynamic_slice_in_dim(
        per_head(conv_bc[0].reshape(lag + 1, 2, G, states), heads), first_head, local_heads, 1
    )
    x_conv = causal_taps(
        jnp.zeros((lag,) + x_heads.shape[1:], jnp.bfloat16), x_heads, empty_ids, all_ids, taps_x
    )
    bc_conv = causal_taps(
        jnp.zeros((lag,) + bc_heads.shape[1:], jnp.bfloat16), bc_heads, empty_ids, all_ids, taps_bc
    )
    bias_heads = lax.dynamic_slice_in_dim(dt_bias[0], first_head, local_heads)
    rates = -jnp.exp(lax.dynamic_slice_in_dim(a_log[0], first_head, local_heads))
    skip = lax.dynamic_slice_in_dim(d_skip[0], first_head, local_heads)
    step_size = jax.nn.softplus(raw_heads.astype(jnp.float32) + bias_heads[None, :])
    _, local = state_space(x_conv, bc_conv, step_size, rates, skip, all_ids)
    attention_mixture = local.astype(jnp.bfloat16)
    mixed_tokens = lax.all_to_all(
        attention_mixture, "ctx", split_axis=0, concat_axis=1, tiled=True
    ).reshape(tokens_here, heads * head_dim)
    gated = mixed_tokens.astype(jnp.float32) * jax.nn.silu(z_in[0].astype(jnp.float32))
    grouped = gated.reshape(tokens_here, G, heads * head_dim // G)
    factor = lax.rsqrt(jnp.mean(grouped * grouped, axis=-1, keepdims=True) + norm_eps)
    mamba_out = (
        (grouped * factor).reshape(tokens_here, heads * head_dim) * norm_gain[0][None, :]
    ).astype(jnp.bfloat16)
    ratio = AH // KVH
    queries = query[0].reshape(tokens_here, KVH, ratio, HD)
    query_pos = place * tokens_here + jnp.arange(tokens_here)
    logit_scale = 1.0 / math.sqrt(HD)
    initial = (
        jnp.full((KVH, ratio, tokens_here), -1e30, jnp.float32),
        jnp.zeros((KVH, ratio, tokens_here), jnp.float32),
        jnp.zeros((KVH, ratio, tokens_here, HD), jnp.float32),
    )
    carry = initial
    key_piece = lax.all_gather(keys[0], "ctx", axis=0, tiled=True)
    value_piece = lax.all_gather(values[0], "ctx", axis=0, tiled=True)
    count = key_piece.shape[0]
    width = math.gcd(count, 512)
    key_blocks = key_piece.reshape(count // width, width, KVH, HD)
    value_blocks = value_piece.reshape(count // width, width, KVH, HD)

    def visit(running, item):
        key_block, value_block, order = item
        first = order * width
        key_ids = lax.dynamic_slice_in_dim(all_ids, first, width)
        key_pos = first + jnp.arange(width)
        allowed = (query_pos[:, None] >= key_pos[None, :]) & (own_ids[:, None] == key_ids[None, :])
        largest, totals, accum = running
        attention_logits = (
            jnp.einsum("tgrd,mgd->grtm", queries, key_block, preferred_element_type=jnp.float32)
            * logit_scale
        )
        masked = jnp.where(allowed, attention_logits, -1e30)
        newest = jnp.maximum(largest, jnp.max(masked, axis=-1))
        weight = jnp.where(allowed, jnp.exp(masked - newest[..., None]), 0.0)
        correct = jnp.exp(largest - newest)
        totals = totals * correct + jnp.sum(weight, axis=-1)
        accum = accum * correct[..., None] + jnp.einsum(
            "grtm,mgd->grtd",
            weight.astype(jnp.bfloat16),
            value_block,
            preferred_element_type=jnp.float32,
        )
        running = (newest, totals, accum)
        return (running, None)

    carry, _ = lax.scan(
        visit, carry, (key_blocks, value_blocks, jnp.arange(count // width, dtype=jnp.int32))
    )
    largest, totals, accum = carry
    attended = accum / totals[..., None]
    attended = (
        jnp.transpose(attended, (2, 0, 1, 3)).reshape(tokens_here, AH * HD).astype(jnp.bfloat16)
    )
    handoff = from_behind(attended, "pipe", 1)
    return (mamba_out[None], handoff[None])


def solution(mesh):
    in_specs = (
        P("pipe", "ctx", None),
        P("pipe", "ctx", None),
        P("pipe", "ctx", None),
        P("pipe", "ctx", None),
        P("pipe", None),
        P("pipe", None),
        P("pipe", None),
        P("pipe", None, None),
        P("pipe", None, None),
        P("pipe", None),
        P("pipe", "ctx"),
        P("pipe", "ctx", None),
        P("pipe", "ctx", None),
        P("pipe", "ctx", None),
    )
    out_specs = (P("pipe", "ctx", None), P("pipe", "ctx", None))
    return jax.shard_map(
        on_device, mesh=mesh, in_specs=in_specs, out_specs=out_specs, check_vma=False
    )
```

profile of v0, /device:TPU:0, one launch (start us, length us, event | category | flops | bytes accessed | tf_op | source)
XLA Modules:
  0.0 315.3 jit_solution(9040418585861244815)
XLA Ops:
  2.2 6.3 %all-to-all-start = ((bf16[8,2,512]{2,1,0:T(2,128)(2,1)}), bf16[8,2,512]{2,1,0:T(2,128)(2,1)S(1)}, u32[]{:S(2)}, u32[]{:S(2)}) async-start(bf16[8,2,512]{2,1,0:T(2,128)(2,1)} %reshape.218), calls=%async_computation | async-start | bytes 32768 | tf_op jit(solution)/shard_map/all_to_all | solution.py:129
  8.5 4.3 %reshape_squeeze.16 = bf16[64,128,64]{2,1,0:T(8,128)(2,1)} reshape(bf16[1,64,8192]{2,1,0:T(8,128)(2,1)} %param.16) | data formatting | bytes 2097152 | tf_op jit(solution)/shard_map/reshape;squeeze | solution.py:125
  18.4 5.1 %all-to-all-start.1 = ((bf16[8,2,32768]{2,1,0:T(2,128)(2,1)}), bf16[8,2,32768]{2,1,0:T(2,128)(2,1)S(1)}, u32[]{:S(2)}, u32[]{:S(2)}) async-start(bf16[8,2,32768]{2,1,0:T(2,128)(2,1)} %reshape.220), calls=%async_computation.1 | async-start | bytes 2097152 | tf_op jit(solution)/shard_map/all_to_all | solution.py:128
  23.7 6.1 %broadcast_in_dim.176 = bf16[64,4,32,2,128]{4,3,0,2,1:T(2,128)(2,1)} broadcast(bf16[64,4,2,128]{3,2,0,1:T(2,128)(2,1)S(1)} %copy.94), dimensions={0,1,3,4} | broadcast | bytes 4325376 | tf_op jit(solution)/shard_map/broadcast_in_dim | solution.py:42
  29.8 7.6 %reshape_reshape.7 = bf16[64,128,256]{2,0,1:T(8,128)(2,1)} reshape(bf16[64,4,32,2,128]{4,3,0,2,1:T(2,128)(2,1)} %broadcast_in_dim.176) | data formatting | bytes 8388608 | tf_op jit(solution)/shard_map/reshape;reshape | solution.py:43
  37.5 12.6 %all-to-all-done.1 = bf16[8,2,32768]{2,1,0:T(2,128)(2,1)S(1)} async-done(((bf16[8,2,32768]{2,1,0:T(2,128)(2,1)}), bf16[8,2,32768]{2,1,0:T(2,128)(2,1)S(1)}, u32[]{:S(2)}, u32[]{:S(2)}) %all-to-all-start.1) | async-done | bytes 1048608 | tf_op jit(solution)/shard_map/all_to_all | solution.py:128
  50.1 4.6 %all-to-all-start.2 = ((bf16[64,128,256]{2,0,1:T(8,128)(2,1)}), bf16[64,128,256]{2,0,1:T(8,128)(2,1)}, u32[]{:S(2)}, u32[]{:S(2)}) async-start(bf16[64,128,256]{2,0,1:T(8,128)(2,1)} %reshape_reshape.7), calls=%async_computation.2 | async-start | bytes 8388608 | tf_op jit(solution)/shard_map/all_to_all | solution.py:130
  56.6 92.2 %all-reduce.3 = s32[512]{0:T(512)S(1)} all-reduce(s32[512]{0:T(512)S(1)} %bitcast_dynamic-update-slice_fusion), channel_id=2, replica_groups=mesh['pipe'=4,'ctx'=8] {'ctx'}, use_global_device_ids=true, to_apply=%add.3 | all-reduce | flops 512 | bytes 4096 | tf_op jit(solution)/shard_map/all_gather | solution.py:122
  148.8 14.2 %all-gather.1 = bf16[1,512,256]{2,1,0:T(8,128)(2,1)S(1)} all-gather(bf16[1,64,256]{2,1,0:T(8,128)(2,1)S(1)} %copy-done.11), channel_id=3, replica_groups=mesh['pipe'=4,'ctx'=8] {'ctx'}, dimensions={1}, use_global_device_ids=true | all-gather | bytes 294912 | tf_op jit(solution)/shard_map/all_gather | solution.py:170
  180.2 4.7 %copy.96 = bf16[8,64,16,256]{3,2,1,0:T(8,128)(2,1)S(1)} copy(bf16[8,64,16,256]{3,1,2,0:T(8,128)(2,1)} %bitcast.17) | data formatting | bytes 8388608 | tf_op jit(solution)/shard_map/all_to_all | solution.py:130
  184.9 7.8 %multiply_convert_fusion = bf16[512,16,256]{2,1,0:T(8,128)(2,1)} fusion(bf16[512,16,256]{2,1,0:T(8,128)(2,1)S(1)} %bitcast.248, f32[16,256]{1,0:T(8,128)S(1)} %get-tuple-element.192, f32[16,256]{1,0:T(8,128)S(1)} %get-tuple-element.190, f32[16,256]{1,0:T(8,128)S(1)} %get-tuple-element.191, f32[16,256]{1,0:T(8,128)S(1)} %get-tuple-element.189, ...), kind=kLoop, calls=%fused_computation.49 | loop fusion | flops 39845888 | bytes 8455680 | tf_op jit(solution)/shard_map/convert_element_type | solution.py:34
  192.7 31.1 %while.3 = (s32[]{:T(128)}, f32[16,64,128]{2,1,0:T(8,128)S(1)}, s32[]{:T(128)}, bf16[2,256,16,64]{1,3,2,0:T(8,128)(2,1)}, s32[2,256]{1,0:T(2,128)S(1)}, /*index=...) while((s32[]{:T(128)}, f32[16,64,128]{2,1,0:T(8,128)S(1)}, ...), condition=%wide.region_3.4_spmd.clone, body=%wide.region_0.3_spmd.clone.sunk | while | flops 882074176 | bytes 19326392 | solution.py:94
  197.0 3.6 %fusion.87 = f32[256,16,64]{0,2,1:T(8,128)} fusion(f32[256,16]{0,1:T(8,128)S(1)} %bitcast.258, f32[256,16]{0,1:T(8,128)S(1)} %bitcast_bitcast_fusion.2, pred[256,256]{0,1:T(8,128)(4,1)S(1)} %fusion.86, bf16[256,16,256]{2,0,1:T(8,128)(2,1)S(1)} %bitcast.242, bf16[2,256,16,64]{1,3,2,0:T(8,128)(2,1)} %get-tuple-element.310, s32[]{:T(128)} %get-tuple-element.289), kind=kOutput, calls=%fused_computation.5.clone.1 | convolution fusion | flops 408944640 | bytes 3785216 | tf_op jit(solution)/shard_map/while/body/eval_jaxpr/tsh,shp->thp/dot_general | solution.py:67
  202.2 3.4 %fusion.88 = bf16[2,256,16,64]{1,3,2,0:T(8,128)(2,1)} fusion(bf16[2,256,16,64]{1,3,2,0:T(8,128)(2,1)} %get-tuple-element.292, s32[]{:T(128)} %get-tuple-element.289, f32[256,16,64]{0,2,1:T(8,128)} %fusion.87, bf16[256,16,256]{2,0,1:T(8,128)(2,1)S(1)} %bitcast.243, f32[16]{0:T(128)S(1)} %get-tuple-element.312, f32[256,16]{0,1:T(8,128)S(1)} %get-tuple-element.274, ...), kind=kOutput, calls=%fused_computation.11.clone.1 | convolution fusion | flops 404094976 | bytes 4211713 | tf_op jit(solution)/shard_map/while/body/eval_jaxpr/thn,hpn->thp/dot_general | solution.py:70
  212.6 3.6 %fusion.87 = f32[256,16,64]{0,2,1:T(8,128)} fusion(f32[256,16]{0,1:T(8,128)S(1)} %bitcast.258, f32[256,16]{0,1:T(8,128)S(1)} %bitcast_bitcast_fusion.2, pred[256,256]{0,1:T(8,128)(4,1)S(1)} %fusion.86, bf16[256,16,256]{2,0,1:T(8,128)(2,1)S(1)} %bitcast.242, bf16[2,256,16,64]{1,3,2,0:T(8,128)(2,1)} %get-tuple-element.310, s32[]{:T(128)} %get-tuple-element.289), kind=kOutput, calls=%fused_computation.5.clone.1 | convolution fusion | flops 408944640 | bytes 3785216 | tf_op jit(solution)/shard_map/while/body/eval_jaxpr/tsh,shp->thp/dot_general | solution.py:67
  229.5 4.6 %all-to-all-start.3 = ((bf16[8,2,32768]{2,1,0:T(2,128)(2,1)}), bf16[8,2,32768]{2,1,0:T(2,128)(2,1)}, u32[]{:S(2)}, u32[]{:S(2)}) async-start(bf16[8,2,32768]{2,1,0:T(2,128)(2,1)} %reshape.222), calls=%async_computation.3 | async-start | bytes 2097152 | tf_op jit(solution)/shard_map/all_to_all | solution.py:151
  236.8 30.7 %all-gather.2 = bf16[1,512,256]{2,1,0:T(8,128)(2,1)S(1)} all-gather(bf16[1,64,256]{2,1,0:T(8,128)(2,1)S(1)} %copy-done.12), channel_id=4, replica_groups=mesh['pipe'=4,'ctx'=8] {'ctx'}, dimensions={1}, use_global_device_ids=true | all-gather | bytes 294912 | tf_op jit(solution)/shard_map/all_gather | solution.py:171
  267.7 3.6 %fusion.32 = f32[4,8,64]{2,1,0:T(8,128)S(1)} fusion(f32[4,512,64,8]{1,2,3,0:T(8,128)} %get-tuple-element.203, f32[4,8,64]{2,1,0:T(8,128)S(1)} %get-tuple-element.198, pred[64,512]{1,0:T(8,128)(4,1)S(1)} %copy-done.3), kind=kLoop, calls=%fused_computation.55 | loop fusion | flops 5240832 | bytes 4243456 | tf_op jit(solution)/shard_map/while/body/eval_jaxpr/reduce_sum | solution.py:192
  278.3 5.5 %copy.105 = f32[64,8,16,64]{0,1,3,2:T(8,128)} copy(f32[64,8,16,64]{3,2,1,0:T(8,128)} %reshape.196) | data formatting | bytes 4194304 | tf_op jit(solution)/shard_map/convert_element_type | solution.py:154
  289.4 4.0 %reshape.198 = f32[8,64,16,64]{1,0,3,2:T(8,128)} reshape(bf16[512,16,64]{0,2,1:T(8,128)(2,1)} %copy.102) | data formatting | bytes 3145728 | tf_op jit(solution)/shard_map/convert_element_type | solution.py:154
  293.4 4.9 %multiply_reduce_fusion = f32[64,8]{0,1:T(8,128)S(1)} fusion(f32[64,8,16,64]{0,1,3,2:T(8,128)} %copy.105, f32[8,64,16,64]{1,0,3,2:T(8,128)} %reshape.198), kind=kLoop, calls=%fused_computation.52 | loop fusion | flops 3669504 | bytes 4196352 | tf_op jit(solution)/shard_map/reduce_sum | solution.py:156
  301.2 6.3 %copy.103 = f32[64,8,16,64]{3,2,1,0:T(8,128)} copy(f32[64,8,16,64]{0,1,3,2:T(8,128)} %bitcast.246) | data formatting | bytes 4194304 | tf_op jit(solution)/shard_map/convert_element_type | solution.py:154
  307.5 3.5 %reshape.195 = f32[1,64,8192]{2,1,0:T(8,128)S(1)} reshape(f32[64,8,16,64]{3,2,1,0:T(8,128)} %copy.103) | data formatting | bytes 4194304 | tf_op jit(solution)/shard_map/convert_element_type | solution.py:154
  311.1 3.5 %multiply_convert_fusion.1 = bf16[1,64,8192]{2,1,0:T(8,128)(2,1)} fusion(f32[1,64,8192]{2,1,0:T(8,128)} %mul.292, f32[1,64,8192]{2,1,0:T(8,128)S(1)} %reshape.195, f32[8192]{0:T(1024)S(1)} %bitcast.262, bf16[1,64,8192]{2,1,0:T(8,128)(2,1)} %param.17), kind=kLoop, calls=%fused_computation.57 | loop fusion | flops 4718592 | bytes 6324224 | tf_op jit(solution)/shard_map/convert_element_type | solution.py:159
  (146 shorter events, 68.1 us)
Async XLA Ops:
  2.2 16.2 %all-to-all-start = ((bf16[8,2,512]{2,1,0:T(2,128)(2,1)}), bf16[8,2,512]{2,1,0:T(2,128)(2,1)S(1)}, u32[]{:S(2)}, u32[]{:S(2)}) async-start(bf16[8,2,512]{2,1,0:T(2,128)(2,1)} %reshape.218), calls=%async_computation | async-start | bytes 32768 | tf_op jit(solution)/shard_map/all_to_all | solution.py:129
  12.7 10.7 %copy-start.5 = (bf16[1,64,1024]{2,1,0:T(8,128)(2,1)S(1)}, bf16[1,64,1024]{2,1,0:T(8,128)(2,1)}, u32[]{:S(2)}) copy-start(bf16[1,64,1024]{2,1,0:T(8,128)(2,1)} %param.18) | copy-start | bytes 393220
  18.4 31.7 %all-to-all-start.1 = ((bf16[8,2,32768]{2,1,0:T(2,128)(2,1)}), bf16[8,2,32768]{2,1,0:T(2,128)(2,1)S(1)}, u32[]{:S(2)}, u32[]{:S(2)}) async-start(bf16[8,2,32768]{2,1,0:T(2,128)(2,1)} %reshape.220), calls=%async_computation.1 | async-start | bytes 2097152 | tf_op jit(solution)/shard_map/all_to_all | solution.py:128
  37.4 17.3 %copy-start.15 = (bf16[1,4,1024]{2,1,0:T(4,128)(2,1)S(1)}, bf16[1,4,1024]{2,1,0:T(4,128)(2,1)}, u32[]{:S(2)}) copy-start(bf16[1,4,1024]{2,1,0:T(4,128)(2,1)} %param.24) | copy-start | bytes 24580
  37.4 17.7 %copy-start.6 = (bf16[1,4,8192]{2,1,0:T(4,128)(2,1)S(1)}, bf16[1,4,8192]{2,1,0:T(4,128)(2,1)}, u32[]{:S(2)}) copy-start(bf16[1,4,8192]{2,1,0:T(4,128)(2,1)} %param.23) | copy-start | bytes 196612
  37.4 17.8 %copy-start.23 = (u32[32]{0:T(128)S(1)}, u32[32]{0:T(128)}, u32[]{:S(2)}) copy-start(u32[32]{0:T(128)} %constant.111) | copy-start | bytes 388
  37.4 19.1 %copy-start.19 = (s32[1,64]{1,0:T(1,128)S(1)}, s32[1,64]{1,0:T(1,128)}, u32[]{:S(2)}) copy-start(s32[1,64]{1,0:T(1,128)} %param.26) | copy-start | bytes 772
  37.4 111.4 %copy-start.11 = (bf16[1,64,256]{2,1,0:T(8,128)(2,1)S(1)}, bf16[1,64,256]{2,1,0:T(8,128)(2,1)}, u32[]{:S(2)}) copy-start(bf16[1,64,256]{2,1,0:T(8,128)(2,1)} %param.28) | copy-start | bytes 98308
  37.4 125.7 %copy-start.4 = (bf16[1,64,2048]{2,1,0:T(8,128)(2,1)S(1)}, bf16[1,64,2048]{2,1,0:T(8,128)(2,1)}, u32[]{:S(2)}) copy-start(bf16[1,64,2048]{2,1,0:T(8,128)(2,1)} %param.27) | copy-start | bytes 786436
  37.4 126.2 %copy-start.22 = (f32[1,128]{1,0:T(1,128)S(1)}, f32[1,128]{1,0:T(1,128)}, u32[]{:S(2)}) copy-start(f32[1,128]{1,0:T(1,128)} %param.20) | copy-start | bytes 1540
  37.5 126.8 %copy-start.20 = (f32[1,128]{1,0:T(1,128)S(1)}, f32[1,128]{1,0:T(1,128)}, u32[]{:S(2)}) copy-start(f32[1,128]{1,0:T(1,128)} %param.21) | copy-start | bytes 1540
  37.5 126.8 %copy-start.21 = (f32[1,128]{1,0:T(1,128)S(1)}, f32[1,128]{1,0:T(1,128)}, u32[]{:S(2)}) copy-start(f32[1,128]{1,0:T(1,128)} %param.22) | copy-start | bytes 1540
  50.1 130.1 %all-to-all-start.2 = ((bf16[64,128,256]{2,0,1:T(8,128)(2,1)}), bf16[64,128,256]{2,0,1:T(8,128)(2,1)}, u32[]{:S(2)}, u32[]{:S(2)}) async-start(bf16[64,128,256]{2,0,1:T(8,128)(2,1)} %reshape_reshape.7), calls=%async_computation.2 | async-start | bytes 8388608 | tf_op jit(solution)/shard_map/all_to_all | solution.py:130
  170.5 6.2 %copy-start.8 = (f32[16,64]{1,0:T(8,128)S(1)}, f32[16,64]{1,0:T(8,128)}, u32[]{:S(2)}) copy-start(f32[16,64]{1,0:T(8,128)} %get-tuple-element.194) | copy-start | bytes 12292
  170.5 6.2 %copy-start.9 = (f32[16,64]{1,0:T(8,128)S(1)}, f32[16,64]{1,0:T(8,128)}, u32[]{:S(2)}) copy-start(f32[16,64]{1,0:T(8,128)} %get-tuple-element.195) | copy-start | bytes 12292
  170.5 6.2 %copy-start.10 = (f32[16,64]{1,0:T(8,128)S(1)}, f32[16,64]{1,0:T(8,128)}, u32[]{:S(2)}) copy-start(f32[16,64]{1,0:T(8,128)} %get-tuple-element.196) | copy-start | bytes 12292
  170.5 6.2 %copy-start.16 = (pred[512]{0:T(512)(128)(4,1)S(1)}, pred[512]{0:T(512)(128)(4,1)}, u32[]{:S(2)}) copy-start(pred[512]{0:T(512)(128)(4,1)} %get-tuple-element.199) | copy-start | bytes 1540
  184.9 7.8 %copy-start.13 = (f32[16]{0:T(128)S(1)}, f32[16]{0:T(128)}, u32[]{:S(2)}) copy-start(f32[16]{0:T(128)} %fusion.63) | copy-start | bytes 196
  200.6 7.0 %copy-start.14 = (f32[16]{0:T(128)S(1)}, f32[16]{0:T(128)}, u32[]{:S(2)}) copy-start(f32[16]{0:T(128)} %get-tuple-element.345) | copy-start | bytes 196 | tf_op jit(solution)/shard_map/while
  216.2 7.0 %copy-start.14 = (f32[16]{0:T(128)S(1)}, f32[16]{0:T(128)}, u32[]{:S(2)}) copy-start(f32[16]{0:T(128)} %get-tuple-element.345) | copy-start | bytes 196 | tf_op jit(solution)/shard_map/while
  223.8 10.3 %copy-start.3 = (pred[64,512]{1,0:T(8,128)(4,1)S(1)}, pred[64,512]{1,0:T(8,128)(4,1)}, u32[]{:S(2)}) copy-start(pred[64,512]{1,0:T(8,128)(4,1)} %fusion.47) | copy-start | bytes 98308
  229.5 7.3 %copy-start.12 = (bf16[1,64,256]{2,1,0:T(8,128)(2,1)S(1)}, bf16[1,64,256]{2,1,0:T(8,128)(2,1)}, u32[]{:S(2)}) copy-start(bf16[1,64,256]{2,1,0:T(8,128)(2,1)} %param.29) | copy-start | bytes 98308
  229.5 54.3 %all-to-all-start.3 = ((bf16[8,2,32768]{2,1,0:T(2,128)(2,1)}), bf16[8,2,32768]{2,1,0:T(2,128)(2,1)}, u32[]{:S(2)}, u32[]{:S(2)}) async-start(bf16[8,2,32768]{2,1,0:T(2,128)(2,1)} %reshape.222), calls=%async_computation.3 | async-start | bytes 2097152 | tf_op jit(solution)/shard_map/all_to_all | solution.py:151
  273.5 10.3 %collective-permute-start = (bf16[64,2048]{1,0:T(8,128)(2,1)S(1)}, bf16[64,2048]{1,0:T(8,128)(2,1)S(1)}, u32[]{:S(2)}, u32[]{:S(2)}) collective-permute-start(bf16[64,2048]{1,0:T(8,128)(2,1)S(1)} %convert_element_type.151), channel_id=1, source_target_pairs={{0,8},{8,16},{16,24},{24,0},{1,9},{9,17},{17,25},{25,1},{2,10},{10... | collective-permute-start | bytes 786440 | tf_op jit(solution)/shard_map/ppermute | solution.py:17
  (6 other events, 28.0 us)
where the time goes:
time: 317 us; the launch traced here: 315 us
  blocking collectives  137 us (43%)
  local copies, waits for them, and re-layouts  89.4 us (28%)
  other arithmetic  28.6 us (9%)
  starting transfers between devices  22.1 us (7%)
  matrix products  21.1 us (7%)
  waiting for transfers between devices  12.6 us (4%)
    all_gather x1, blocking collectives, on_device(): all_ids = lax.all_gather(own_ids, 'ctx', axis=0, tiled=True)  92.2 us
    all_gather x1, blocking collectives, on_device(): value_piece = lax.all_gather(values[0], 'ctx', axis=0, tiled=True)  30.7 us
    unnamed x57, local copies, waits for them, and re-layouts  14.6 us
    all_gather x1, blocking collectives, on_device(): key_piece = lax.all_gather(keys[0], 'ctx', axis=0, tiled=True)  14.2 us
    convert_element_type x3, local copies, waits for them, and re-layouts, on_device(): mixed_tokens.astype(jnp.float32) * jax.nn.silu(z_in[0].astype(jnp.float32))  13.9 us
    all_to_all x1, waiting for transfers between devices, on_device(): lax.all_to_all(x_send, 'ctx', split_axis=1, concat_axis=0, tiled=True)  12.6 us
    convert_element_type x2, other arithmetic, causal_taps(): return jax.nn.silu(summed).astype(jnp.bfloat16)  10 us
    convert_element_type x2, local copies, waits for them, and re-layouts, on_device(): z_in[0].astype(jnp.float32)  8.7 us
  transfers between devices with their start and end apart: 5, of which 1 were waited for; matrix products, arithmetic and copies ran while one was open for 18% of the time, Pallas kernels for 0%

commit v1 on v0

--- a/solution.py
+++ b/solution.py
@@ -1,3 +1,4 @@
+import functools
 import math
 import jax
 import jax.numpy as jnp
@@ -9,6 +10,37 @@
 KVH = 4
 HD = 64
 norm_eps = 1e-05
+
+
+def _supply_all_edge(raw, which_dim):
+    raw = jnp.moveaxis(raw, 0, which_dim)
+    out_arr = raw.shape
+    return raw.reshape(
+        *out_arr[:which_dim], out_arr[which_dim] * out_arr[which_dim + 1], *out_arr[which_dim + 2 :]
+    )
+
+
+def spread_edge_on_mesh(body, axis_id):
+    outcome_arr = lax.axis_size(axis_id)
+    x_new = lax.axis_index(axis_id)
+    y2, part_now = (outcome_arr, x_new)
+    r1, k_now = (body[None], 1)
+    while k_now < y2:
+        piece_out = lax.ppermute(r1, axis_id, [(dd, dd ^ k_now) for dd in range(y2)])
+        taken_in = part_now & k_now == 0
+        r1 = jnp.concatenate(
+            [jnp.where(taken_in, r1, piece_out), jnp.where(taken_in, piece_out, r1)]
+        )
+        k_now *= 2
+    return r1
+
+
+def enter_values(s0, message, axis_k):
+    z2 = spread_edge_on_mesh(s0, message)
+    return _supply_all_edge(z2, axis_k)
+
+
+mix_tables_on_mesh = functools.partial(enter_values, message="ctx", axis_k=0)
 
 
 def from_behind(value, axis, steps):
@@ -167,7 +199,7 @@
         jnp.zeros((KVH, ratio, tokens_here, HD), jnp.float32),
     )
     carry = initial
-    key_piece = lax.all_gather(keys[0], "ctx", axis=0, tiled=True)
+    key_piece = mix_tables_on_mesh(keys[0])
     value_piece = lax.all_gather(values[0], "ctx", axis=0, tiled=True)
     count = key_piece.shape[0]
     width = math.gcd(count, 512)

time: 317 us -> 298 us (0.940)
  blocking collectives: 137 us -> 106 us
  waiting for transfers between devices: 12.6 us -> 35 us
  other arithmetic: 28.6 us -> 23.2 us
  local copies, waits for them, and re-layouts: 89.4 us -> 85.6 us
    all_gather x1, blocking collectives: 30.7 us -> 14.2 us  [on_device(): value_piece = lax.all_gather(values[0], 'ctx', axis=0, tiled=True)]
    all_gather x1 -> x0, blocking collectives: 14.2 us -> none  [on_device(): key_piece = lax.all_gather(keys[0], 'ctx', axis=0, tiled=True)]
    ppermute x0 -> x3, waiting for transfers between devices: none -> 12.1 us  [spread_edge_on_mesh(): lax.ppermute(r1, axis_id, [(dd, dd ^ k_now) for dd in range(y2)])]
    all_to_all x1, waiting for transfers between devices: 0.01 us -> 10.3 us  [on_device(): lax.all_to_all(attention_mixture, 'ctx', split_axis=0, concat_axis=1, til...]
    unnamed x57 -> x41, local copies, waits for them, and re-layouts: 14.6 us -> 12.9 us
  transfers between devices with their start and end apart: 5 -> 8, of which waited for: 1 -> 4; matrix products, arithmetic and copies ran while one was open for 18% -> 18% of each run, Pallas kernels for 0% -> 0%
where the time goes in v1:
time: 298 us; the launch traced here: 297 us
  blocking collectives  106 us (36%)
  local copies, waits for them, and re-layouts  85.6 us (29%)
  waiting for transfers between devices  35 us (12%)
  other arithmetic  23.2 us (8%)
  starting transfers between devices  22.4 us (8%)
  matrix products  20.4 us (7%)
    all_gather x1, blocking collectives, on_device(): all_ids = lax.all_gather(own_ids, 'ctx', axis=0, tiled=True)  91.9 us
    all_gather x1, blocking collectives, on_device(): value_piece = lax.all_gather(values[0], 'ctx', axis=0, tiled=True)  14.2 us
    unnamed x41, local copies, waits for them, and re-layouts  12.9 us
    all_to_all x1, waiting for transfers between devices, on_device(): lax.all_to_all(x_send, 'ctx', split_axis=1, concat_axis=0, tiled=True)  12.6 us
    convert_element_type x3, local copies, waits for them, and re-layouts, on_device(): mixed_tokens.astype(jnp.float32) * jax.nn.silu(z_in[0].astype(jnp.float32))  12.3 us
    ppermute x3, waiting for transfers between devices, spread_edge_on_mesh(): lax.ppermute(r1, axis_id, [(dd, dd ^ k_now) for dd in range(y2)])  12.1 us
    all_to_all x1, waiting for transfers between devices, on_device(): lax.all_to_all(attention_mixture, 'ctx', split_axis=0, concat_axis=1, til...  10.3 us
    convert_element_type x2, other arithmetic, causal_taps(): return jax.nn.silu(summed).astype(jnp.bfloat16)  10 us
  transfers between devices with their start and end apart: 8, of which 4 were waited for; matrix products, arithmetic and copies ran while one was open for 18% of the time, Pallas kernels for 0%

profile of v1, /device:TPU:0, one launch (start us, length us, event | category | flops | bytes accessed | tf_op | source)
XLA Modules:
  0.0 297.1 jit_solution(4981214089558017275)
XLA Ops:
  2.2 6.3 %all-to-all-start = ((bf16[8,2,512]{2,1,0:T(2,128)(2,1)}), bf16[8,2,512]{2,1,0:T(2,128)(2,1)S(1)}, u32[]{:S(2)}, u32[]{:S(2)}) async-start(bf16[8,2,512]{2,1,0:T(2,128)(2,1)} %reshape.216), calls=%async_computation | async-start | bytes 32768 | tf_op jit(solution)/shard_map/all_to_all | solution.py:161
  8.5 4.2 %reshape_squeeze.16 = bf16[64,128,64]{2,1,0:T(8,128)(2,1)} reshape(bf16[1,64,8192]{2,1,0:T(8,128)(2,1)} %param.16) | data formatting | bytes 2097152 | tf_op jit(solution)/shard_map/reshape;squeeze | solution.py:157
  18.4 5.1 %all-to-all-start.1 = ((bf16[8,2,32768]{2,1,0:T(2,128)(2,1)}), bf16[8,2,32768]{2,1,0:T(2,128)(2,1)S(1)}, u32[]{:S(2)}, u32[]{:S(2)}) async-start(bf16[8,2,32768]{2,1,0:T(2,128)(2,1)} %reshape.218), calls=%async_computation.1 | async-start | bytes 2097152 | tf_op jit(solution)/shard_map/all_to_all | solution.py:160
  23.7 6.1 %broadcast_in_dim.176 = bf16[64,4,32,2,128]{4,3,0,2,1:T(2,128)(2,1)} broadcast(bf16[64,4,2,128]{3,2,0,1:T(2,128)(2,1)S(1)} %copy.94), dimensions={0,1,3,4} | broadcast | bytes 4325376 | tf_op jit(solution)/shard_map/broadcast_in_dim | solution.py:74
  29.8 7.6 %reshape_reshape.8 = bf16[64,128,256]{2,0,1:T(8,128)(2,1)} reshape(bf16[64,4,32,2,128]{4,3,0,2,1:T(2,128)(2,1)} %broadcast_in_dim.176) | data formatting | bytes 8388608 | tf_op jit(solution)/shard_map/reshape;reshape | solution.py:75
  37.5 12.6 %all-to-all-done.1 = bf16[8,2,32768]{2,1,0:T(2,128)(2,1)S(1)} async-done(((bf16[8,2,32768]{2,1,0:T(2,128)(2,1)}), bf16[8,2,32768]{2,1,0:T(2,128)(2,1)S(1)}, u32[]{:S(2)}, u32[]{:S(2)}) %all-to-all-start.1) | async-done | bytes 1048608 | tf_op jit(solution)/shard_map/all_to_all | solution.py:160
  50.1 4.6 %all-to-all-start.2 = ((bf16[64,128,256]{2,0,1:T(8,128)(2,1)}), bf16[64,128,256]{2,0,1:T(8,128)(2,1)}, u32[]{:S(2)}, u32[]{:S(2)}) async-start(bf16[64,128,256]{2,0,1:T(8,128)(2,1)} %reshape_reshape.8), calls=%async_computation.2 | async-start | bytes 8388608 | tf_op jit(solution)/shard_map/all_to_all | solution.py:162
  56.9 91.9 %all-reduce.3 = s32[512]{0:T(512)S(1)} all-reduce(s32[512]{0:T(512)S(1)} %bitcast_dynamic-update-slice_fusion), channel_id=2, replica_groups=mesh['pipe'=4,'ctx'=8] {'ctx'}, use_global_device_ids=true, to_apply=%add.3 | all-reduce | flops 512 | bytes 4096 | tf_op jit(solution)/shard_map/all_gather | solution.py:154
  148.9 14.2 %all-gather.1 = bf16[1,512,256]{2,1,0:T(8,128)(2,1)S(1)} all-gather(bf16[1,64,256]{2,1,0:T(8,128)(2,1)S(1)} %copy-done.7), channel_id=3, replica_groups=mesh['pipe'=4,'ctx'=8] {'ctx'}, dimensions={1}, use_global_device_ids=true | all-gather | bytes 294912 | tf_op jit(solution)/shard_map/all_gather | solution.py:203
  165.2 4.2 %collective-permute-done.1 = bf16[2,64,256]{2,1,0:T(8,128)(2,1)S(1)} collective-permute-done((bf16[2,64,256]{2,1,0:T(8,128)(2,1)S(1)}, bf16[2,64,256]{2,1,0:T(8,128)(2,1)S(1)}, u32[]{:S(2)}, u32[]{:S(2)}) %collective-permute-start.1) | collective-permute-done | bytes 65568 | tf_op jit(solution)/shard_map/ppermute | solution.py:29
  170.3 7.9 %collective-permute-done.2 = bf16[4,64,256]{2,1,0:T(8,128)(2,1)S(1)} collective-permute-done((bf16[4,64,256]{2,1,0:T(8,128)(2,1)S(1)}, bf16[4,64,256]{2,1,0:T(8,128)(2,1)S(1)}, u32[]{:S(2)}, u32[]{:S(2)}) %collective-permute-start.2) | collective-permute-done | bytes 131104 | tf_op jit(solution)/shard_map/ppermute | solution.py:29
  191.9 4.7 %copy.96 = bf16[8,64,16,256]{3,2,1,0:T(8,128)(2,1)S(1)} copy(bf16[8,64,16,256]{3,1,2,0:T(8,128)(2,1)} %bitcast.17) | data formatting | bytes 8388608 | tf_op jit(solution)/shard_map/all_to_all | solution.py:162
  196.7 7.8 %multiply_convert_fusion = bf16[512,16,256]{2,1,0:T(8,128)(2,1)} fusion(bf16[512,16,256]{2,1,0:T(8,128)(2,1)S(1)} %bitcast.243, f32[16,256]{1,0:T(8,128)S(1)} %get-tuple-element.194, f32[16,256]{1,0:T(8,128)S(1)} %get-tuple-element.192, f32[16,256]{1,0:T(8,128)S(1)} %get-tuple-element.193, f32[16,256]{1,0:T(8,128)S(1)} %get-tuple-element.191, ...), kind=kLoop, calls=%fused_computation.49 | loop fusion | flops 39845888 | bytes 8455680 | tf_op jit(solution)/shard_map/convert_element_type | solution.py:66
  204.5 29.6 %while.3 = (s32[]{:T(128)}, f32[16,64,128]{2,1,0:T(8,128)S(1)}, s32[]{:T(128)}, bf16[2,256,16,64]{1,3,2,0:T(8,128)(2,1)}, s32[2,256]{1,0:T(2,128)S(1)}, /*index=...) while((s32[]{:T(128)}, f32[16,64,128]{2,1,0:T(8,128)S(1)}, ...), condition=%wide.region_3.4_spmd.clone, body=%wide.region_0.3_spmd.clone.sunk | while | flops 882074176 | bytes 19326100 | solution.py:126
  208.0 3.6 %fusion.87 = f32[256,16,64]{0,2,1:T(8,128)} fusion(f32[256,16]{0,1:T(8,128)S(1)} %bitcast.253, f32[256,16]{0,1:T(8,128)S(1)} %bitcast_bitcast_fusion.2, pred[256,256]{0,1:T(8,128)(4,1)S(1)} %fusion.86, bf16[256,16,256]{2,0,1:T(8,128)(2,1)S(1)} %bitcast.237, bf16[2,256,16,64]{1,3,2,0:T(8,128)(2,1)} %get-tuple-element.316, s32[]{:T(128)} %get-tuple-element.295), kind=kOutput, calls=%fused_computation.5.clone.1 | convolution fusion | flops 408944640 | bytes 3785216 | tf_op jit(solution)/shard_map/while/body/eval_jaxpr/tsh,shp->thp/dot_general | solution.py:99
  213.2 3.4 %fusion.88 = bf16[2,256,16,64]{1,3,2,0:T(8,128)(2,1)} fusion(bf16[2,256,16,64]{1,3,2,0:T(8,128)(2,1)} %get-tuple-element.298, s32[]{:T(128)} %get-tuple-element.295, f32[256,16,64]{0,2,1:T(8,128)} %fusion.87, bf16[256,16,256]{2,0,1:T(8,128)(2,1)S(1)} %bitcast.238, f32[16]{0:T(128)S(1)} %get-tuple-element.318, f32[256,16]{0,1:T(8,128)S(1)} %get-tuple-element.280, ...), kind=kOutput, calls=%fused_computation.11.clone.1 | convolution fusion | flops 404094976 | bytes 4211713 | tf_op jit(solution)/shard_map/while/body/eval_jaxpr/thn,hpn->thp/dot_general | solution.py:102
  222.8 3.6 %fusion.87 = f32[256,16,64]{0,2,1:T(8,128)} fusion(f32[256,16]{0,1:T(8,128)S(1)} %bitcast.253, f32[256,16]{0,1:T(8,128)S(1)} %bitcast_bitcast_fusion.2, pred[256,256]{0,1:T(8,128)(4,1)S(1)} %fusion.86, bf16[256,16,256]{2,0,1:T(8,128)(2,1)S(1)} %bitcast.237, bf16[2,256,16,64]{1,3,2,0:T(8,128)(2,1)} %get-tuple-element.316, s32[]{:T(128)} %get-tuple-element.295), kind=kOutput, calls=%fused_computation.5.clone.1 | convolution fusion | flops 408944640 | bytes 3785216 | tf_op jit(solution)/shard_map/while/body/eval_jaxpr/tsh,shp->thp/dot_general | solution.py:99
  228.0 3.4 %fusion.88 = bf16[2,256,16,64]{1,3,2,0:T(8,128)(2,1)} fusion(bf16[2,256,16,64]{1,3,2,0:T(8,128)(2,1)} %get-tuple-element.298, s32[]{:T(128)} %get-tuple-element.295, f32[256,16,64]{0,2,1:T(8,128)} %fusion.87, bf16[256,16,256]{2,0,1:T(8,128)(2,1)S(1)} %bitcast.238, f32[16]{0:T(128)S(1)} %get-tuple-element.318, f32[256,16]{0,1:T(8,128)S(1)} %get-tuple-element.280, ...), kind=kOutput, calls=%fused_computation.11.clone.1 | convolution fusion | flops 404094976 | bytes 4211713 | tf_op jit(solution)/shard_map/while/body/eval_jaxpr/thn,hpn->thp/dot_general | solution.py:102
  239.7 3.8 %all-to-all-start.3 = ((bf16[8,2,32768]{2,1,0:T(2,128)(2,1)}), bf16[8,2,32768]{2,1,0:T(2,128)(2,1)S(1)}, u32[]{:S(2)}, u32[]{:S(2)}) async-start(bf16[8,2,32768]{2,1,0:T(2,128)(2,1)} %reshape.220), calls=%async_computation.3 | async-start | bytes 2097152 | tf_op jit(solution)/shard_map/all_to_all | solution.py:183
  254.0 5.5 %copy.105 = f32[64,8,16,64]{0,1,3,2:T(8,128)} copy(f32[64,8,16,64]{3,2,1,0:T(8,128)} %reshape.195) | data formatting | bytes 4194304 | tf_op jit(solution)/shard_map/convert_element_type | solution.py:186
  259.5 10.3 %all-to-all-done.3 = bf16[8,2,32768]{2,1,0:T(2,128)(2,1)S(1)} async-done(((bf16[8,2,32768]{2,1,0:T(2,128)(2,1)}), bf16[8,2,32768]{2,1,0:T(2,128)(2,1)S(1)}, u32[]{:S(2)}, u32[]{:S(2)}) %all-to-all-start.3) | async-done | bytes 1048608 | tf_op jit(solution)/shard_map/all_to_all | solution.py:183
  275.3 4.9 %multiply_reduce_fusion = f32[64,8]{0,1:T(8,128)S(1)} fusion(f32[64,8,16,64]{0,1,3,2:T(8,128)} %copy.105, f32[8,64,16,64]{1,0,3,2:T(8,128)} %reshape.197), kind=kLoop, calls=%fused_computation.52 | loop fusion | flops 3669504 | bytes 4196352 | tf_op jit(solution)/shard_map/reduce_sum | solution.py:188
  283.2 6.3 %copy.103 = f32[64,8,16,64]{3,2,1,0:T(8,128)} copy(f32[64,8,16,64]{0,1,3,2:T(8,128)} %bitcast.241) | data formatting | bytes 4194304 | tf_op jit(solution)/shard_map/convert_element_type | solution.py:186
  289.5 3.6 %reshape.194 = f32[1,64,8192]{2,1,0:T(8,128)S(1)} reshape(f32[64,8,16,64]{3,2,1,0:T(8,128)} %copy.103) | data formatting | bytes 4194304 | tf_op jit(solution)/shard_map/convert_element_type | solution.py:186
  (137 shorter events, 67.0 us)
Async XLA Ops:
  2.2 16.2 %all-to-all-start = ((bf16[8,2,512]{2,1,0:T(2,128)(2,1)}), bf16[8,2,512]{2,1,0:T(2,128)(2,1)S(1)}, u32[]{:S(2)}, u32[]{:S(2)}) async-start(bf16[8,2,512]{2,1,0:T(2,128)(2,1)} %reshape.216), calls=%async_computation | async-start | bytes 32768 | tf_op jit(solution)/shard_map/all_to_all | solution.py:161
  12.7 10.7 %copy-start.4 = (bf16[1,64,1024]{2,1,0:T(8,128)(2,1)S(1)}, bf16[1,64,1024]{2,1,0:T(8,128)(2,1)}, u32[]{:S(2)}) copy-start(bf16[1,64,1024]{2,1,0:T(8,128)(2,1)} %param.18) | copy-start | bytes 393220
  18.4 31.7 %all-to-all-start.1 = ((bf16[8,2,32768]{2,1,0:T(2,128)(2,1)}), bf16[8,2,32768]{2,1,0:T(2,128)(2,1)S(1)}, u32[]{:S(2)}, u32[]{:S(2)}) async-start(bf16[8,2,32768]{2,1,0:T(2,128)(2,1)} %reshape.218), calls=%async_computation.1 | async-start | bytes 2097152 | tf_op jit(solution)/shard_map/all_to_all | solution.py:160
  37.4 17.2 %copy-start.8 = (bf16[1,64,256]{2,1,0:T(8,128)(2,1)S(1)}, bf16[1,64,256]{2,1,0:T(8,128)(2,1)}, u32[]{:S(2)}) copy-start(bf16[1,64,256]{2,1,0:T(8,128)(2,1)} %param.28) | copy-start | bytes 98308
  37.4 17.6 %copy-start.9 = (bf16[1,4,1024]{2,1,0:T(4,128)(2,1)S(1)}, bf16[1,4,1024]{2,1,0:T(4,128)(2,1)}, u32[]{:S(2)}) copy-start(bf16[1,4,1024]{2,1,0:T(4,128)(2,1)} %param.24) | copy-start | bytes 24580
  37.4 18.0 %copy-start.5 = (bf16[1,4,8192]{2,1,0:T(4,128)(2,1)S(1)}, bf16[1,4,8192]{2,1,0:T(4,128)(2,1)}, u32[]{:S(2)}) copy-start(bf16[1,4,8192]{2,1,0:T(4,128)(2,1)} %param.23) | copy-start | bytes 196612
  37.4 18.1 %copy-start.14 = (u32[32]{0:T(128)S(1)}, u32[32]{0:T(128)}, u32[]{:S(2)}) copy-start(u32[32]{0:T(128)} %constant.117) | copy-start | bytes 388
  37.4 19.4 %copy-start.10 = (s32[1,64]{1,0:T(1,128)S(1)}, s32[1,64]{1,0:T(1,128)}, u32[]{:S(2)}) copy-start(s32[1,64]{1,0:T(1,128)} %param.26) | copy-start | bytes 772
  37.4 111.4 %copy-start.11 = (f32[1,128]{1,0:T(1,128)S(1)}, f32[1,128]{1,0:T(1,128)}, u32[]{:S(2)}) copy-start(f32[1,128]{1,0:T(1,128)} %param.21) | copy-start | bytes 1540
  37.5 111.3 %copy-start.12 = (f32[1,128]{1,0:T(1,128)S(1)}, f32[1,128]{1,0:T(1,128)}, u32[]{:S(2)}) copy-start(f32[1,128]{1,0:T(1,128)} %param.22) | copy-start | bytes 1540
  37.5 111.4 %copy-start.7 = (bf16[1,64,256]{2,1,0:T(8,128)(2,1)S(1)}, bf16[1,64,256]{2,1,0:T(8,128)(2,1)}, u32[]{:S(2)}) copy-start(bf16[1,64,256]{2,1,0:T(8,128)(2,1)} %param.29) | copy-start | bytes 98308
  37.5 125.8 %copy-start.13 = (f32[1,128]{1,0:T(1,128)S(1)}, f32[1,128]{1,0:T(1,128)}, u32[]{:S(2)}) copy-start(f32[1,128]{1,0:T(1,128)} %param.20) | copy-start | bytes 1540
  37.5 125.9 %copy-start.3 = (bf16[1,64,2048]{2,1,0:T(8,128)(2,1)S(1)}, bf16[1,64,2048]{2,1,0:T(8,128)(2,1)}, u32[]{:S(2)}) copy-start(bf16[1,64,2048]{2,1,0:T(8,128)(2,1)} %param.27) | copy-start | bytes 786436
  50.1 4.9 %copy-start = (bf16[8,2,32768]{2,1,0:T(2,128)(2,1)}, bf16[8,2,32768]{2,1,0:T(2,128)(2,1)S(1)}, u32[]{:S(2)}) copy-start(bf16[8,2,32768]{2,1,0:T(2,128)(2,1)S(1)} %all-to-all-done.1) | copy-start | bytes 3145732
  50.1 141.8 %all-to-all-start.2 = ((bf16[64,128,256]{2,0,1:T(8,128)(2,1)}), bf16[64,128,256]{2,0,1:T(8,128)(2,1)}, u32[]{:S(2)}, u32[]{:S(2)}) async-start(bf16[64,128,256]{2,0,1:T(8,128)(2,1)} %reshape_reshape.8), calls=%async_computation.2 | async-start | bytes 8388608 | tf_op jit(solution)/shard_map/all_to_all | solution.py:162
  54.7 110.3 %collective-permute-start = (bf16[1,64,256]{2,1,0:T(8,128)(2,1)S(1)}, bf16[1,64,256]{2,1,0:T(8,128)(2,1)S(1)}, u32[]{:S(2)}, u32[]{:S(2)}) collective-permute-start(bf16[1,64,256]{2,1,0:T(8,128)(2,1)S(1)} %copy-done.8), channel_id=1, source_target_pairs={{0,1},{1,0},{2,3},{3,2},{4,5},{5,4},{6,7},{7,6},{8,9},{9,8},{10,11... | collective-permute-start | bytes 98312 | tf_op jit(solution)/shard_map/ppermute | solution.py:29
  165.0 4.4 %collective-permute-start.1 = (bf16[2,64,256]{2,1,0:T(8,128)(2,1)S(1)}, bf16[2,64,256]{2,1,0:T(8,128)(2,1)S(1)}, u32[]{:S(2)}, u32[]{:S(2)}) collective-permute-start(bf16[2,64,256]{2,1,0:T(8,128)(2,1)S(1)} %pad_maximum_fusion.2), channel_id=1, source_target_pairs={{0,2},{1,3},{2,0},{3,1},{4,6},{5,7},{6,4},{7,5},{8,10},{9,11},{10,... | collective-permute-start | bytes 196616 | tf_op jit(solution)/shard_map/ppermute | solution.py:29
  169.5 8.7 %collective-permute-start.2 = (bf16[4,64,256]{2,1,0:T(8,128)(2,1)S(1)}, bf16[4,64,256]{2,1,0:T(8,128)(2,1)S(1)}, u32[]{:S(2)}, u32[]{:S(2)}) collective-permute-start(bf16[4,64,256]{2,1,0:T(8,128)(2,1)S(1)} %pad_maximum_fusion.1), channel_id=1, source_target_pairs={{0,4},{1,5},{2,6},{3,7},{4,0},{5,1},{6,2},{7,3},{8,12},{9,13},{10,... | collective-permute-start | bytes 393224 | tf_op jit(solution)/shard_map/ppermute | solution.py:29
  239.7 30.1 %all-to-all-start.3 = ((bf16[8,2,32768]{2,1,0:T(2,128)(2,1)}), bf16[8,2,32768]{2,1,0:T(2,128)(2,1)S(1)}, u32[]{:S(2)}, u32[]{:S(2)}) async-start(bf16[8,2,32768]{2,1,0:T(2,128)(2,1)} %reshape.220), calls=%async_computation.3 | async-start | bytes 2097152 | tf_op jit(solution)/shard_map/all_to_all | solution.py:183
  246.9 3.8 %copy-start.1 = (bf16[1,64,8192]{2,1,0:T(8,128)(2,1)S(1)}, bf16[1,64,8192]{2,1,0:T(8,128)(2,1)}, u32[]{:S(2)}) copy-start(bf16[1,64,8192]{2,1,0:T(8,128)(2,1)} %param.17) | copy-start | bytes 3145732
  249.2 10.2 %collective-permute-start.3 = (bf16[64,2048]{1,0:T(8,128)(2,1)S(1)}, bf16[64,2048]{1,0:T(8,128)(2,1)S(1)}, u32[]{:S(2)}, u32[]{:S(2)}) collective-permute-start(bf16[64,2048]{1,0:T(8,128)(2,1)S(1)} %convert_element_type.151), channel_id=1, source_target_pairs={{0,8},{8,16},{16,24},{24,0},{1,9},{9,17},{17,25},{25,1},{2,10},{10... | collective-permute-start | bytes 786440 | tf_op jit(solution)/shard_map/ppermute | solution.py:49
  289.5 3.6 %copy-start.2 = (bf16[1,64,8192]{2,1,0:T(8,128)(2,1)S(1)}, bf16[1,64,8192]{2,1,0:T(8,128)(2,1)}, u32[]{:S(2)}) copy-start(bf16[1,64,8192]{2,1,0:T(8,128)(2,1)} %param.17) | copy-start | bytes 3145732
  289.5 3.6 %copy-start.6 = (f32[1,8192]{1,0:T(1,128)S(1)}, f32[1,8192]{1,0:T(1,128)}, u32[]{:S(2)}) copy-start(f32[1,8192]{1,0:T(1,128)} %param.25) | copy-start | bytes 98308
